TPU v7x, 32 devices: a whole 2x2x4 slice. The times are simulated.
32 devices in a mesh: freq: 2 (over y), shot: 4 (over z), surf: 4 (over x, core).
Axes of the slice: x: 2, y: 2, z: 4, core: 2. Of those that a mesh axis runs over, the one named last changes fastest.
Arguments:
- spectra: bfloat16 [256, 2, 64, 128], P(('freq', 'shot', 'surf')), parts along dimension 0, may hold values from -6 to 6
- block_site: int32 [128, 64], P(('shot', 'surf')), may hold values from 0 to 63, as said below
- live_traces: int32 [128, 64], P(('shot', 'surf')), may hold values from 64 to 128
- taper_class: int32 [128, 64], P(('shot', 'surf')), may hold values from 0 to 7
- taper_table: float32 [8, 128], replicated, may hold values from 0.2 to 1
- operator: bfloat16 [4, 8192, 2048], P('freq', 'shot', 'surf'), parts along dimension 0, may hold values from -0.0625 to 0.0625
Outputs:
- multiples: float32 [256, 2, 2048], P(('freq', 'shot'), None, 'surf'), parts along dimension 0
There are 2 independent parts, one for each index of `freq`. A program takes and returns all parts, laid end to end along the dimension named above; an argument that names none is the same for every part. Nothing has to cross between parts.
Inputs may be any that keep to these rules, and one draw needn't show every extreme that they name: `block_site`: the 64 entries of a shot are distinct surface blocks, 16 in each of 4 surface groups (group = block // 16). All 8 consecutive shots that one device holds, at index i along shot, record in the same groups (i + j + k) mod 4, k from 0 to 3, with one j of 0 to 0 for the device. So every device has exactly 128 blocks in each of its 4 groups.
All inputs are finite; a program needn't handle non-finite values.
Results may differ from a plain program's by a relative error of at most 0.0029.
Values may be sent and summed in bfloat16 or wider, within the bound.
A program may use at most 128 MiB of HBM per device.

v0:
```python
import jax
import jax.numpy as jnp
from jax import lax
from jax.sharding import PartitionSpec as P


def taper_weights(taper_class, live_traces, taper_table, traces):
    classes = taper_table.shape[0]
    onehot = (
        taper_class[:, :, None] == jnp.arange(classes, dtype=jnp.int32)[None, None, :]
    ).astype(jnp.float32)
    weights = jnp.einsum("sbc,ct->sbt", onehot, taper_table, precision=lax.Precision.HIGHEST)
    trace_lane = jnp.arange(traces, dtype=jnp.int32)
    return jnp.where(trace_lane[None, None, :] < live_traces[:, :, None], weights, 0.0)


def group_multiples(data_grid, operator):
    products = jnp.einsum(
        "ugsck,dkr->guscdr", data_grid, operator, preferred_element_type=jnp.float32
    )
    real_part = products[:, :, :, 0, 0] - products[:, :, :, 1, 1]
    imag_part = products[:, :, :, 0, 1] + products[:, :, :, 1, 0]
    return jnp.stack([real_part, imag_part], axis=3).reshape(-1, 2, operator.shape[2])


def local(spectra, block_site, live_traces, taper_class, taper_table, operator):
    local_shots = spectra.shape[0]
    traces = spectra.shape[3]
    groups = lax.axis_size("shot")
    columns = lax.axis_size("surf")
    group_blocks = operator.shape[1] // traces
    weights = taper_weights(taper_class, live_traces, taper_table, traces)
    tapered = (spectra.astype(jnp.float32) * weights[:, None]).astype(jnp.bfloat16)
    total_blocks = groups * group_blocks
    shot_rows = jnp.arange(local_shots, dtype=jnp.int32)[:, None, None]
    component = jnp.arange(2, dtype=jnp.int32)[None, :, None]
    dense_grid = jnp.zeros((local_shots, 2, total_blocks, traces), jnp.bfloat16)
    dense_grid = dense_grid.at[shot_rows, component, block_site[:, None, :]].set(tapered)
    received = lax.all_to_all(
        dense_grid.reshape(local_shots, 2, total_blocks * traces),
        "shot",
        split_axis=2,
        concat_axis=0,
        tiled=True,
    )
    spectra_all = lax.all_gather(received[None], "surf", axis=0, tiled=True)
    data_grid = spectra_all.reshape(columns, groups, local_shots, 2, group_blocks * traces)
    result = lax.psum_scatter(
        group_multiples(data_grid, operator), "shot", scatter_dimension=0, tiled=True
    )
    return result


def solution(mesh):
    return jax.shard_map(
        local,
        mesh=mesh,
        in_specs=(
            P(("freq", "shot", "surf"), None, None, None),
            P(("shot", "surf"), None),
            P(("shot", "surf"), None),
            P(("shot", "surf"), None),
            P(),
            P("freq", "shot", "surf"),
        ),
        out_specs=P(("freq", "shot"), None, "surf"),
        check_vma=False,
    )
```

profile of v0, /device:TPU:0, one launch (start us, length us, event | category | flops | bytes accessed | tf_op | source)
XLA Modules:
  0.0 109.2 jit_solution(17701137517075543345)
XLA Ops:
  6.5 0.0 copy-start
  6.5 0.0 all-gather.2.cloned.1.call-start
  6.5 0.7 compare_select_fusion
  7.3 0.7 and_reduce_fusion
  8.0 0.7 multiply_reduce_fusion
  8.7 0.1 reshape.74
  8.8 0.0 copy-done
  8.8 1.1 %convolution_select_fusion = f32[8,64,128]{2,1,0:T(8,128)S(1)} fusion(s32[8,64]{1,0:T(8,128)} %param.8, s32[8,64]{1,0:T(8,128)} %param.9, f32[8,128]{1,0:T(8,128)S(1)} %copy-done), kind=kOutput, calls=%fused_computation.4 | convolution fusion | flops 6426624 | bytes 270336 | tf_op jit(solution)/shard_map/sbc,ct->sbt/dot_general | solution.py:12
  9.9 1.0 multiply_convert_fusion
  11.0 3.2 %scatter_custom_fusion = bf16[1024,128]{1,0:T(8,128)(2,1)S(1)} fusion(s32[1024]{0:T(1024)S(1)} %reshape.74, bf16[1024,128]{1,0:T(8,128)(2,1)S(1)} %bitcast.35, bf16[]{:T(256)} %constant.4.clone.1), kind=kCustom, calls=%fused_computation.12 | custom fusion | bytes 262146
  14.2 0.1 reshape.67
  14.3 6.8 %copy.37 = bf16[8,2,8192]{0,1,2:T(2,128)(2,1)} copy(bf16[8,2,8192]{2,1,0:T(2,128)(2,1)S(1)} %reshape.67) | data formatting | bytes 524288 | tf_op jit(solution)/shard_map/reshape | solution.py:40
  21.1 5.8 %reshape.85 = bf16[4,2,16384]{2,1,0:T(2,128)(2,1)S(1)} reshape(bf16[8192,2,8]{2,1,0:T(2,128)(2,1)} %bitcast.29) | data formatting | bytes 524288
  26.8 15.0 %all_to_all.15 = bf16[4,2,16384]{2,1,0:T(2,128)(2,1)S(1)} all-to-all(bf16[4,2,16384]{2,1,0:T(2,128)(2,1)S(1)} %reshape.85), channel_id=1, replica_groups=mesh['freq'=2,'shot'=4,'surf'=4] {'shot'}, dimensions={0} | all-to-all | bytes 524288 | tf_op jit(solution)/shard_map/all_to_all | solution.py:39
  41.8 5.9 %reshape.86 = bf16[8192,2,8]{2,1,0:T(2,128)(2,1)} reshape(bf16[4,2,16384]{2,1,0:T(2,128)(2,1)S(1)} %all_to_all.15) | data formatting | bytes 524288
  47.8 9.5 %copy.46 = bf16[8,2,4,2048]{3,2,0,1:T(4,128)(2,1)S(1)} copy(bf16[8,2,4,2048]{0,1,3,2:T(2,128)(2,1)} %bitcast.30) | data formatting | bytes 524288 | tf_op jit(solution)/shard_map/all_to_all | solution.py:39
  57.3 0.9 copy.52
  58.2 0.0 all-gather.2.cloned.1.call-update
  58.2 0.0 reduce-scatter.2.cloned.1.call-start
  58.2 15.9 %all-gather.2.cloned.1.call-done = bf16[4,32,2,2048]{3,1,2,0:T(8,128)(2,1)} async-done(((bf16[1,32,2,2048]{3,1,2,0:T(8,128)(2,1)}), bf16[4,32,2,2048]{3,1,2,0:T(8,128)(2,1)}) %all-gather.2.cloned.1.call-update) | async-done | bytes 1048592 | tf_op jit(solution)/shard_map/all_gather | solution.py:46
  74.2 3.8 %fusion.2 = f32[4,4,8,2,2,512]{5,2,4,3,0,1:T(8,128)S(1)} fusion(bf16[2,2048,512]{2,1,0:T(8,128)(2,1)} %param.11, bf16[4,32,2,2048]{3,1,2,0:T(8,128)(2,1)} %all-gather.2.cloned.1.call-done), kind=kOutput, calls=%fused_computation.3 | convolution fusion | flops 1073741824 | bytes 6291456 | tf_op jit(solution)/shard_map/ugsck,dkr->guscdr/dot_general | solution.py:18
  77.9 0.1 slice_subtract_fusion
  78.1 0.8 pad_maximum_fusion
  78.9 0.0 reduce-scatter.2.cloned.1.call-update
  78.9 21.8 %reduce-scatter.2.cloned.1.call-done = f32[32,2,512]{2,0,1:T(8,128)} async-done(((f32[128,2,512]{2,0,1:T(8,128)}), f32[32,2,512]{2,0,1:T(8,128)}) %reduce-scatter.2.cloned.1.call-update) | async-done | bytes 131088 | tf_op jit(solution)/shard_map/reduce_scatter | solution.py:48
  100.7 1.7 %copy.43 = f32[32,2,512]{2,1,0:T(2,128)} copy(f32[32,2,512]{2,0,1:T(8,128)} %reduce-scatter.2.cloned.1.call-done) | data formatting | bytes 262144 | tf_op jit(solution)/shard_map/reduce_scatter | solution.py:48
  (7 shorter events, 0.1 us)
Async XLA Ops:
  6.5 2.3 %copy-start = (f32[8,128]{1,0:T(8,128)S(1)}, f32[8,128]{1,0:T(8,128)}, u32[]{:S(2)}) copy-start(f32[8,128]{1,0:T(8,128)} %param.10) | copy-start | bytes 12292
  6.5 67.6 %all-gather.2.cloned.1.call-start = ((), (), s32[]{:S(2)}) async-start(), calls=%async_computation.2 | async-start | bytes 1310720 | tf_op jit(solution)/shard_map/all_gather | solution.py:46
  58.2 42.6 %reduce-scatter.2.cloned.1.call-start = ((), (), s32[]{:S(2)}) async-start(), calls=%async_computation.3 | async-start | bytes 655360 | tf_op jit(solution)/shard_map/reduce_scatter | solution.py:48
Sparse Core Ops, SparseCore 0:
  58.3 15.8 all-gather.1
  79.1 21.6 reduce-scatter.1
where the time goes:
time: 110 us; the launch traced here: 109 us
  waiting for transfers between devices  37.8 us (34%)
  local copies, waits for them, and re-layouts  34 us (31%)
  blocking collectives  15 us (14%)
  between operations  13.5 us (12%)
  matrix products  4.87 us (4%)
  other arithmetic  4.1 us (4%)
    reduce_scatter x1, waiting for transfers between devices, local(): lax.psum_scatter(group_multiples(data_grid, operator), 'shot', scatter_di...  21.8 us
    all_gather x1, waiting for transfers between devices, local(): spectra_all = lax.all_gather(received[None], 'surf', axis=0, tiled=True)  15.9 us
    unnamed x7, local copies, waits for them, and re-layouts  15 us
    all_to_all x1, blocking collectives, local(): lax.all_to_all(dense_grid.reshape(local_shots, 2, total_blocks * traces),...  15 us
    all_to_all x2, local copies, waits for them, and re-layouts, local(): lax.all_to_all(dense_grid.reshape(local_shots, 2, total_blocks * traces),...  10.4 us
    reshape x2, local copies, waits for them, and re-layouts, local(): dense_grid.reshape(local_shots, 2, total_blocks * traces)  6.87 us
    dot_general x1, matrix products, group_multiples(): jnp.einsum('ugsck,dkr->guscdr', data_grid, operator, preferred_element_ty...  3.76 us
  transfers between devices with their start and end apart: 2, of which 2 were waited for; matrix products, arithmetic and copies ran while one was open for 0% of the time, Pallas kernels for 0%

commit v1 on v0

v1 whole, which is shorter than its diff:
```python
import functools

import jax
import jax.numpy as jnp
from jax import lax
from jax.experimental import pallas as pl
from jax.experimental.pallas import tpu as pltpu
from jax.sharding import PartitionSpec as P

MESH = pl.DeviceIdType.MESH
PIECES = 1


def flip(index, bits, size):
    total, unit = 0, 1
    while unit < size:
        total = total + unit * (((index // unit) % 2 + (bits // unit) % 2) % 2)
        unit *= 2
    return total


def kernel(
    groups, columns,
    spectra_hbm, site_hbm, live_hbm, class_hbm, table_hbm, operator_hbm, out_ref,
    spectra, site, live, classes, table, operator,
    outgoing, data, near_out, near_in, far_out, far_in,
    load_sem, z_send, z_recv, x_send, x_recv, c_send, c_recv, near_send, near_recv, far_send, far_recv,
):
    me = lax.axis_index("shot")
    column = lax.axis_index("surf")
    across = flip(column, 2, columns)
    beside = flip(column, 1, columns)
    neighbour = flip(me, 1, groups)
    shots, _, blocks, traces = spectra.shape
    tapers = table.shape[0]
    group_blocks = operator.shape[1] // traces
    piece_blocks = group_blocks // PIECES
    depth = piece_blocks * traces
    receivers = operator.shape[2]

    def load(source, target, slot):
        return pltpu.make_async_copy(source, target, load_sem.at[slot])

    small = [
        load(spectra_hbm, spectra, 0),
        load(site_hbm, site, 1),
        load(live_hbm, live, 2),
        load(class_hbm, classes, 3),
        load(table_hbm, table, 4),
    ]
    large = load(operator_hbm, operator, 5)
    for copy in small:
        copy.start()
    large.start()

    barrier = pltpu.get_barrier_semaphore()
    for k in range(1, groups):
        pl.semaphore_signal(barrier, inc=1, device_id={"shot": flip(me, k, groups)}, device_id_type=MESH)
    for partner in (across, beside):
        pl.semaphore_signal(barrier, inc=1, device_id={"surf": partner}, device_id_type=MESH)

    for copy in small:
        copy.wait()

    lane = lax.broadcasted_iota(jnp.int32, (shots, shots * blocks), 1)
    row = lax.broadcasted_iota(jnp.int32, (shots, shots * blocks), 0)
    own = lane // blocks == row
    sites = jnp.where(own, jnp.concatenate([site[...]] * shots, axis=1), -1)
    codes = (classes[...] * 256 + live[...]).astype(jnp.float32)
    codes = jnp.concatenate([codes] * shots, axis=1)
    values = jnp.concatenate(
        [spectra[:, c].reshape(shots * blocks, traces) for c in range(2)], axis=1
    )
    trace_lane = lax.broadcasted_iota(jnp.int32, (group_blocks, shots, traces), 2)

    def place(group):
        point = lax.broadcasted_iota(jnp.int32, (group_blocks, shots, shots * blocks), 0)
        hit = sites[None] == point + group * group_blocks
        pick = jnp.where(hit, 1.0, 0.0).reshape(group_blocks * shots, shots * blocks)
        placed = jnp.dot(pick.astype(jnp.bfloat16), values, preferred_element_type=jnp.float32)
        placed = placed.reshape(group_blocks, shots, 2 * traces)
        code = jnp.sum(jnp.where(hit, codes[None], 0.0), axis=2, keepdims=True).astype(jnp.int32)
        code = jnp.broadcast_to(code, trace_lane.shape)
        taper = code // 256
        weights = jnp.zeros(trace_lane.shape, jnp.float32)
        for k in range(tapers):
            weights = jnp.where(taper == k, table[k : k + 1, :][None], weights)
        weights = jnp.where(trace_lane < code % 256, weights, 0.0)
        return jnp.concatenate(
            [placed[:, :, :traces] * weights, placed[:, :, traces:] * weights], axis=1
        ).astype(jnp.bfloat16)

    def write(placed, target):
        for b in range(group_blocks):
            h, at = b // piece_blocks, (b % piece_blocks) * traces
            target(h)[:, at : at + traces] = placed[b]

    def z_copy(k, h):
        return pltpu.make_async_remote_copy(
            src_ref=outgoing.at[k, h], dst_ref=data.at[me, h, column],
            send_sem=z_send.at[k, h], recv_sem=z_recv.at[k, h],
            device_id={"shot": flip(me, k, groups)}, device_id_type=MESH,
        )

    def z_arrival(k, h):
        other = flip(me, k, groups)
        return pltpu.make_async_remote_copy(
            src_ref=outgoing.at[k, h], dst_ref=data.at[other, h, column],
            send_sem=z_send.at[k, h], recv_sem=z_recv.at[k, h],
            device_id={"shot": other}, device_id_type=MESH,
        )

    def x_copy(k, h, owner):
        slot = data.at[flip(me, k, groups), h, owner]
        return pltpu.make_async_remote_copy(
            src_ref=slot, dst_ref=slot,
            send_sem=x_send.at[k, h], recv_sem=x_recv.at[k, h],
            device_id={"surf": across}, device_id_type=MESH,
        )

    def c_copy(k, h, forwarded, owner):
        slot = data.at[flip(me, k, groups), h, owner]
        return pltpu.make_async_remote_copy(
            src_ref=slot, dst_ref=slot,
            send_sem=c_send.at[k, h, forwarded], recv_sem=c_recv.at[k, h, forwarded],
            device_id={"surf": beside}, device_id_type=MESH,
        )

    def pass_on(k, h):
        x_copy(k, h, column).start()
        c_copy(k, h, 0, column).start()

    def arrive(k, h):
        z_arrival(k, h).wait_recv()
        pass_on(k, h)

    def relay(k, h):
        x_copy(k, h, across).wait_recv()
        c_copy(k, h, 1, across).start()

    def share(k):
        real = imag = 0.0
        for h in range(PIECES):
            c_copy(k, h, 0, beside).wait_recv()
            c_copy(k, h, 1, flip(across, 1, columns)).wait_recv()
            rows = data[flip(me, k, groups), h].reshape(columns * 2 * shots, depth)
            at = h * depth
            real += jnp.dot(rows, operator[0, at : at + depth, :], preferred_element_type=jnp.float32)
            imag += jnp.dot(rows, operator[1, at : at + depth, :], preferred_element_type=jnp.float32)
        real = real.reshape(columns, 2, shots, receivers)
        imag = imag.reshape(columns, 2, shots, receivers)
        return jnp.concatenate(
            [(real[:, 0] - imag[:, 1])[:, None], (imag[:, 0] + real[:, 1])[:, None]], axis=1
        ).reshape(columns * 2 * shots, receivers)

    def near_copy(j):
        return pltpu.make_async_remote_copy(
            src_ref=near_out.at[j], dst_ref=near_in.at[j],
            send_sem=near_send.at[j], recv_sem=near_recv.at[j],
            device_id={"shot": neighbour}, device_id_type=MESH,
        )

    def far_copy(j):
        return pltpu.make_async_remote_copy(
            src_ref=far_out.at[j], dst_ref=far_in.at[j],
            send_sem=far_send.at[j], recv_sem=far_recv.at[j],
            device_id={"shot": flip(me, 2 * j, groups)}, device_id_type=MESH,
        )

    def share_near(j):
        near_out[j] = share(2 * j + 1).astype(jnp.bfloat16)
        near_copy(j).start()

    def share_far(j):
        mine = share(2 * j)
        near_copy(j).wait_recv()
        far_out[j] = (mine + near_in[j].astype(jnp.float32)).astype(jnp.bfloat16)
        far_copy(j).start()

    def share_own():
        out_ref[...] = share(0)

    def send_group(k):
        write(place(flip(me, k, groups)), lambda h: outgoing.at[k, h])
        for h in range(PIECES):
            z_copy(k, h).start()

    pieces = range(PIECES)
    if groups <= 4:
        order = [3, 2, 1][3 - (groups - 1) :]
        first = True
        for k in order:
            write(place(flip(me, k, groups)), lambda h: outgoing.at[k, h])
            if first:
                pl.semaphore_wait(barrier, groups + 1)
                first = False
            for h in pieces:
                z_copy(k, h).start()
        write(place(me), lambda h: data.at[me, h, column])
        for h in pieces:
            pass_on(0, h)
        for h in pieces:
            relay(0, h)
        large.wait()
        share_own()
        if groups == 4:
            for k in (1, 3, 2):
                for h in pieces:
                    arrive(k, h)
                if k == 3:
                    for h in pieces:
                        relay(1, h)
                    share_near(0)
            for h in pieces:
                relay(3, h)
            for h in pieces:
                relay(2, h)
            share_near(1)
            share_far(1)
        else:
            for h in pieces:
                arrive(1, h)
            for h in pieces:
                relay(1, h)
            share_near(0)
    else:
        pl.semaphore_wait(barrier, groups + 1)
        pl.loop(1, groups)(send_group)
        write(place(me), lambda h: data.at[me, h, column])

        for h in pieces:
            pass_on(0, h)

        @pl.loop(1, groups)
        def _(k):
            for h in pieces:
                arrive(k, h)

        @pl.loop(0, groups)
        def _(k):
            for h in pieces:
                relay(k, h)

        large.wait()
        share_own()
        share_near(0)

        @pl.loop(1, groups // 2)
        def _(j):
            share_near(j)
            share_far(j)

    near_copy(0).wait_recv()
    out_ref[...] += near_in[0].astype(jnp.float32)

    def collect(j):
        far_copy(j).wait_recv()
        out_ref[...] += far_in[j].astype(jnp.float32)

    def drain(k):
        for h in pieces:
            x_copy(k, h, column).wait_send()
            c_copy(k, h, 0, column).wait_send()
            c_copy(k, h, 1, across).wait_send()

    def drain_z(k):
        for h in pieces:
            z_copy(k, h).wait_send()

    def repeat(first, last, body):
        if groups <= 4:
            for k in range(first, last):
                body(k)
        else:
            pl.loop(first, last)(body)

    repeat(1, groups // 2, collect)
    repeat(0, groups, drain)
    repeat(1, groups, drain_z)
    repeat(0, groups // 2, lambda j: near_copy(j).wait_send())
    repeat(1, groups // 2, lambda j: far_copy(j).wait_send())


def local(spectra, block_site, live_traces, taper_class, taper_table, operator):
    groups = lax.axis_size("shot")
    columns = lax.axis_size("surf")
    shots, _, _, traces = spectra.shape
    depth = operator.shape[1] // PIECES
    receivers = operator.shape[2]
    rows = columns * 2 * shots
    halves = groups // 2
    dma = pltpu.SemaphoreType.DMA
    result = pl.pallas_call(
        functools.partial(kernel, groups, columns),
        out_shape=jax.ShapeDtypeStruct((rows, receivers), jnp.float32),
        in_specs=[pl.BlockSpec(memory_space=pl.ANY)] * 6,
        out_specs=pl.BlockSpec(memory_space=pltpu.VMEM),
        scratch_shapes=[
            pltpu.VMEM(spectra.shape, spectra.dtype),
            pltpu.VMEM(block_site.shape, jnp.int32),
            pltpu.VMEM(live_traces.shape, jnp.int32),
            pltpu.VMEM(taper_class.shape, jnp.int32),
            pltpu.VMEM(taper_table.shape, jnp.float32),
            pltpu.VMEM(operator.shape, operator.dtype),
            pltpu.VMEM((groups, PIECES, 2 * shots, depth), jnp.bfloat16),
            pltpu.VMEM((groups, PIECES, columns, 2 * shots, depth), jnp.bfloat16),
            pltpu.VMEM((halves, rows, receivers), jnp.bfloat16),
            pltpu.VMEM((halves, rows, receivers), jnp.bfloat16),
            pltpu.VMEM((halves, rows, receivers), jnp.bfloat16),
            pltpu.VMEM((halves, rows, receivers), jnp.bfloat16),
            dma((6,)),
            dma((groups, PIECES)),
            dma((groups, PIECES)),
            dma((groups, PIECES)),
            dma((groups, PIECES)),
            dma((groups, PIECES, 2)),
            dma((groups, PIECES, 2)),
            dma((halves,)),
            dma((halves,)),
            dma((halves,)),
            dma((halves,)),
        ],
        compiler_params=pltpu.CompilerParams(
            collective_id=0, has_side_effects=True, vmem_limit_bytes=48 * 2**20
        ),
    )(spectra, block_site, live_traces, taper_class, taper_table, operator)
    result = result.reshape(columns, 2, shots, receivers)
    return result.transpose(0, 2, 1, 3).reshape(columns * shots, 2, receivers)


def solution(mesh):
    return jax.shard_map(
        local,
        mesh=mesh,
        in_specs=(
            P(("freq", "shot", "surf"), None, None, None),
            P(("shot", "surf"), None),
            P(("shot", "surf"), None),
            P(("shot", "surf"), None),
            P(),
            P("freq", "shot", "surf"),
        ),
        out_specs=P(("freq", "shot"), None, "surf"),
        check_vma=False,
    )
```

time: 110 us -> 33.9 us (0.31)
  waiting for transfers between devices: 37.8 us -> 0 us
  local copies, waits for them, and re-layouts: 34 us -> 6.64 us
  Pallas kernels: 0 us -> 26.9 us
  blocking collectives: 15 us -> 0 us
  between operations: 13.5 us -> 0.02 us
  matrix products: 4.87 us -> 0 us
  other arithmetic: 4.1 us -> 0 us
    pallas_call x0 -> x1, Pallas kernels: none -> 26.9 us  [local(): pl.pallas_call(functools.partial(kernel, groups, columns), out_shape=jax....]
    reduce_scatter x1 -> x0, waiting for transfers between devices: 21.8 us -> none  [local(): lax.psum_scatter(group_multiples(data_grid, operator), 'shot', scatter_di...]
    all_gather x1 -> x0, waiting for transfers between devices: 15.9 us -> none  [local(): spectra_all = lax.all_gather(received[None], 'surf', axis=0, tiled=True)]
    all_to_all x1 -> x0, blocking collectives: 15 us -> none  [local(): lax.all_to_all(dense_grid.reshape(local_shots, 2, total_blocks * traces),...]
    all_to_all x2 -> x0, local copies, waits for them, and re-layouts: 10.4 us -> none  [local(): lax.all_to_all(dense_grid.reshape(local_shots, 2, total_blocks * traces),...]
    unnamed x7 -> x12, local copies, waits for them, and re-layouts: 15 us -> 5.88 us
    reshape x2 -> x0, local copies, waits for them, and re-layouts: 6.87 us -> none  [local(): dense_grid.reshape(local_shots, 2, total_blocks * traces)]
    dot_general x2 -> x0, matrix products: 4.87 us -> none  [the longest x1 3.76 us: group_multiples(): jnp.einsum('ugsck,dkr->guscdr', data_grid, operator, preferred_element_ty...]
  transfers between devices with their start and end apart: 2 -> 0, of which waited for: 2 -> 0; matrix products, arithmetic and copies ran while one was open for 0% -> 0% of each run, Pallas kernels for 0% -> 0%
where the time goes in v1:
time: 33.9 us; the launch traced here: 33.6 us
  Pallas kernels  26.9 us (79%)
  local copies, waits for them, and re-layouts  6.64 us (20%)
    pallas_call x1, Pallas kernels, local(): pl.pallas_call(functools.partial(kernel, groups, columns), out_shape=jax....  26.9 us
    unnamed x12, local copies, waits for them, and re-layouts  5.88 us
    transpose x1, local copies, waits for them, and re-layouts, local(): return result.transpose(0, 2, 1, 3).reshape(columns * shots, 2, receivers)  0.76 us

profile of v1, /device:TPU:0, one launch (start us, length us, event | category | flops | bytes accessed | tf_op | source)
XLA Modules:
  0.0 33.6 jit_solution(9469793169668362206)
XLA Ops:
  0.0 0.0 copy-start
  0.0 2.2 %copy-done = bf16[2,2048,512]{2,1,0:T(8,128)(2,1)S(1)} copy-done((bf16[2,2048,512]{2,1,0:T(8,128)(2,1)S(1)}, bf16[2,2048,512]{2,1,0:T(8,128)(2,1)}, u32[]{:S(2)}) %copy-start) | copy-done | bytes 4194328
  2.2 0.0 copy-start.1
  2.2 0.9 %copy-done.1 = bf16[8,2,64,128]{3,2,1,0:T(8,128)(2,1)S(1)} copy-done((bf16[8,2,64,128]{3,2,1,0:T(8,128)(2,1)S(1)}, bf16[8,2,64,128]{3,2,1,0:T(8,128)(2,1)}, u32[]{:S(2)}) %copy-start.1) | copy-done | bytes 262168
  3.1 0.0 copy-start.2
  3.1 0.7 %copy-done.2 = s32[8,64]{1,0:T(8,128)S(1)} copy-done((s32[8,64]{1,0:T(8,128)S(1)}, s32[8,64]{1,0:T(8,128)}, u32[]{:S(2)}) %copy-start.2) | copy-done | bytes 2072
  3.8 0.0 copy-start.3
  3.8 0.7 %copy-done.3 = s32[8,64]{1,0:T(8,128)S(1)} copy-done((s32[8,64]{1,0:T(8,128)S(1)}, s32[8,64]{1,0:T(8,128)}, u32[]{:S(2)}) %copy-start.3) | copy-done | bytes 2072
  4.5 0.0 copy-start.4
  4.5 0.7 %copy-done.4 = s32[8,64]{1,0:T(8,128)S(1)} copy-done((s32[8,64]{1,0:T(8,128)S(1)}, s32[8,64]{1,0:T(8,128)}, u32[]{:S(2)}) %copy-start.4) | copy-done | bytes 2072
  5.2 0.0 copy-start.5
  5.2 0.7 %copy-done.5 = f32[8,128]{1,0:T(8,128)S(1)} copy-done((f32[8,128]{1,0:T(8,128)S(1)}, f32[8,128]{1,0:T(8,128)}, u32[]{:S(2)}) %copy-start.5) | copy-done | bytes 4120
  5.9 26.9 %shard_map.64 = f32[64,512]{1,0:T(8,128)S(1)} custom-call(bf16[8,2,64,128]{3,2,1,0:T(8,128)(2,1)S(1)} %copy-done.1, s32[8,64]{1,0:T(8,128)S(1)} %copy-done.2, s32[8,64]{1,0:T(8,128)S(1)} %copy-done.3, s32[8,64]{1,0:T(8,128)S(1)} %copy-done.4, f32[8,128]{1,0:T(8,128)S(1)} %copy-done.5, bf16[2,2048,512]{2,1,0:T(8,128)(2,1)S(1)} %copy-done), custom_call_target="tpu_custom_call" | custom-call | tf_op jit(solution)/shard_map/pallas_call | solution.py:293
  32.8 0.8 %copy.7 = f32[4,8,2,512]{3,2,1,0:T(2,128)} copy(f32[4,8,2,512]{3,1,2,0:T(8,128)S(1)} %bitcast.4) | data formatting | bytes 262144 | tf_op jit(solution)/shard_map/transpose | solution.py:328
Async XLA Ops:
  0.0 2.2 %copy-start = (bf16[2,2048,512]{2,1,0:T(8,128)(2,1)S(1)}, bf16[2,2048,512]{2,1,0:T(8,128)(2,1)}, u32[]{:S(2)}) copy-start(bf16[2,2048,512]{2,1,0:T(8,128)(2,1)} %operator_hbm.1) | copy-start | bytes 12582916
  2.2 0.9 %copy-start.1 = (bf16[8,2,64,128]{3,2,1,0:T(8,128)(2,1)S(1)}, bf16[8,2,64,128]{3,2,1,0:T(8,128)(2,1)}, u32[]{:S(2)}) copy-start(bf16[8,2,64,128]{3,2,1,0:T(8,128)(2,1)} %spectra_hbm.1) | copy-start | bytes 786436
  3.1 0.7 %copy-start.2 = (s32[8,64]{1,0:T(8,128)S(1)}, s32[8,64]{1,0:T(8,128)}, u32[]{:S(2)}) copy-start(s32[8,64]{1,0:T(8,128)} %site_hbm.1) | copy-start | bytes 6148
  3.8 0.7 %copy-start.3 = (s32[8,64]{1,0:T(8,128)S(1)}, s32[8,64]{1,0:T(8,128)}, u32[]{:S(2)}) copy-start(s32[8,64]{1,0:T(8,128)} %live_hbm.1) | copy-start | bytes 6148
  4.5 0.7 %copy-start.4 = (s32[8,64]{1,0:T(8,128)S(1)}, s32[8,64]{1,0:T(8,128)}, u32[]{:S(2)}) copy-start(s32[8,64]{1,0:T(8,128)} %class_hbm.1) | copy-start | bytes 6148
  5.2 0.7 %copy-start.5 = (f32[8,128]{1,0:T(8,128)S(1)}, f32[8,128]{1,0:T(8,128)}, u32[]{:S(2)}) copy-start(f32[8,128]{1,0:T(8,128)} %table_hbm.1) | copy-start | bytes 12292

commit v2 on v1

--- a/solution.py
+++ b/solution.py
@@ -9,6 +9,24 @@
 
 MESH = pl.DeviceIdType.MESH
 PIECES = 1
+SENDS = (1, 0, 2, 3)
+STEPS = (
+    ("relay", 0, 0),
+    ("arrive", 1, 0),
+    ("arrive", 2, 0),
+    ("multiply", 0, 0),
+    ("keep", 0, 0),
+    ("relay", 1, 0),
+    ("arrive", 3, 0),
+    ("relay", 2, 0),
+    ("multiply", 1, 0),
+    ("send", 1, 0),
+    ("relay", 3, 0),
+    ("multiply", 2, 0),
+    ("send", 2, 0),
+    ("multiply", 3, 0),
+    ("send", 3, 0),
+)
 
 
 def flip(index, bits, size):
@@ -21,16 +39,15 @@
 
 def kernel(
     groups, columns,
-    spectra_hbm, site_hbm, live_hbm, class_hbm, table_hbm, operator_hbm, out_ref,
+    spectra_hbm, site_hbm, live_hbm, class_hbm, table_hbm, operator_hbm, own_hbm, incoming_hbm,
     spectra, site, live, classes, table, operator,
-    outgoing, data, near_out, near_in, far_out, far_in,
-    load_sem, z_send, z_recv, x_send, x_recv, c_send, c_recv, near_send, near_recv, far_send, far_recv,
+    outgoing, data, share_out, own_share,
+    load_sem, z_send, z_recv, x_send, x_recv, c_send, c_recv, share_send, share_recv,
 ):
     me = lax.axis_index("shot")
     column = lax.axis_index("surf")
     across = flip(column, 2, columns)
     beside = flip(column, 1, columns)
-    neighbour = flip(me, 1, groups)
     shots, _, blocks, traces = spectra.shape
     tapers = table.shape[0]
     group_blocks = operator.shape[1] // traces
@@ -138,47 +155,41 @@
         x_copy(k, h, across).wait_recv()
         c_copy(k, h, 1, across).start()
 
+    def products(k, h):
+        c_copy(k, h, 0, beside).wait_recv()
+        c_copy(k, h, 1, flip(across, 1, columns)).wait_recv()
+        rows = data[flip(me, k, groups), h].reshape(columns * 2 * shots, depth)
+        at = h * depth
+        return [
+            jnp.dot(rows, operator[d, at : at + depth, :], preferred_element_type=jnp.float32)
+            for d in range(2)
+        ]
+
+    def combine(parts):
+        first, second = [
+            sum(part[d] for part in parts).reshape(columns, 2, shots, receivers) for d in range(2)
+        ]
+        return jnp.concatenate(
+            [(first[:, 0] - second[:, 1])[:, None], (second[:, 0] + first[:, 1])[:, None]], axis=1
+        ).reshape(columns * 2 * shots, receivers)
+
     def share(k):
-        real = imag = 0.0
-        for h in range(PIECES):
-            c_copy(k, h, 0, beside).wait_recv()
-            c_copy(k, h, 1, flip(across, 1, columns)).wait_recv()
-            rows = data[flip(me, k, groups), h].reshape(columns * 2 * shots, depth)
-            at = h * depth
-            real += jnp.dot(rows, operator[0, at : at + depth, :], preferred_element_type=jnp.float32)
-            imag += jnp.dot(rows, operator[1, at : at + depth, :], preferred_element_type=jnp.float32)
-        real = real.reshape(columns, 2, shots, receivers)
-        imag = imag.reshape(columns, 2, shots, receivers)
-        return jnp.concatenate(
-            [(real[:, 0] - imag[:, 1])[:, None], (imag[:, 0] + real[:, 1])[:, None]], axis=1
-        ).reshape(columns * 2 * shots, receivers)
-
-    def near_copy(j):
-        return pltpu.make_async_remote_copy(
-            src_ref=near_out.at[j], dst_ref=near_in.at[j],
-            send_sem=near_send.at[j], recv_sem=near_recv.at[j],
-            device_id={"shot": neighbour}, device_id_type=MESH,
-        )
-
-    def far_copy(j):
-        return pltpu.make_async_remote_copy(
-            src_ref=far_out.at[j], dst_ref=far_in.at[j],
-            send_sem=far_send.at[j], recv_sem=far_recv.at[j],
-            device_id={"shot": flip(me, 2 * j, groups)}, device_id_type=MESH,
-        )
-
-    def share_near(j):
-        near_out[j] = share(2 * j + 1).astype(jnp.bfloat16)
-        near_copy(j).start()
-
-    def share_far(j):
-        mine = share(2 * j)
-        near_copy(j).wait_recv()
-        far_out[j] = (mine + near_in[j].astype(jnp.float32)).astype(jnp.bfloat16)
-        far_copy(j).start()
-
-    def share_own():
-        out_ref[...] = share(0)
+        return combine([products(k, h) for h in range(PIECES)])
+
+    def share_copy(k):
+        return pltpu.make_async_remote_copy(
+            src_ref=share_out.at[k - 1], dst_ref=incoming_hbm.at[k - 1],
+            send_sem=share_send.at[k], recv_sem=share_recv.at[k],
+            device_id={"shot": flip(me, k, groups)}, device_id_type=MESH,
+        )
+
+    def send_share(k, mine):
+        share_out[k - 1] = mine.astype(jnp.bfloat16)
+        share_copy(k).start()
+
+    def keep_share(mine):
+        own_share[...] = mine
+        load(own_share, own_hbm, 6).start()
 
     def send_group(k):
         write(place(flip(me, k, groups)), lambda h: outgoing.at[k, h])
@@ -186,43 +197,37 @@
             z_copy(k, h).start()
 
     pieces = range(PIECES)
-    if groups <= 4:
-        order = [3, 2, 1][3 - (groups - 1) :]
-        first = True
-        for k in order:
-            write(place(flip(me, k, groups)), lambda h: outgoing.at[k, h])
-            if first:
+    if groups == 4:
+        done = {k: [] for k in range(groups)}
+
+        def multiply(k, h):
+            done[k].append(products(k, h))
+
+        for position, k in enumerate(SENDS):
+            if k == 0:
+                write(place(me), lambda h: data.at[me, h, column])
+            else:
+                write(place(flip(me, k, groups)), lambda h: outgoing.at[k, h])
+            if position == 0:
                 pl.semaphore_wait(barrier, groups + 1)
-                first = False
             for h in pieces:
-                z_copy(k, h).start()
-        write(place(me), lambda h: data.at[me, h, column])
-        for h in pieces:
-            pass_on(0, h)
-        for h in pieces:
-            relay(0, h)
-        large.wait()
-        share_own()
-        if groups == 4:
-            for k in (1, 3, 2):
-                for h in pieces:
-                    arrive(k, h)
-                if k == 3:
-                    for h in pieces:
-                        relay(1, h)
-                    share_near(0)
-            for h in pieces:
-                relay(3, h)
-            for h in pieces:
-                relay(2, h)
-            share_near(1)
-            share_far(1)
-        else:
-            for h in pieces:
-                arrive(1, h)
-            for h in pieces:
-                relay(1, h)
-            share_near(0)
+                if k == 0:
+                    pass_on(0, h)
+                else:
+                    z_copy(k, h).start()
+        for step, k, h in STEPS:
+            if step == "arrive":
+                arrive(k, h)
+            elif step == "relay":
+                relay(k, h)
+            elif step == "multiply":
+                if k == 0 and h == 0:
+                    large.wait()
+                multiply(k, h)
+            elif step == "send":
+                send_share(k, combine(done[k]))
+            elif step == "keep":
+                keep_share(combine(done[k]))
     else:
         pl.semaphore_wait(barrier, groups + 1)
         pl.loop(1, groups)(send_group)
@@ -242,20 +247,11 @@
                 relay(k, h)
 
         large.wait()
-        share_own()
-        share_near(0)
-
-        @pl.loop(1, groups // 2)
-        def _(j):
-            share_near(j)
-            share_far(j)
-
-    near_copy(0).wait_recv()
-    out_ref[...] += near_in[0].astype(jnp.float32)
-
-    def collect(j):
-        far_copy(j).wait_recv()
-        out_ref[...] += far_in[j].astype(jnp.float32)
+        keep_share(share(0))
+
+        @pl.loop(1, groups)
+        def _(k):
+            send_share(k, share(k))
 
     def drain(k):
         for h in pieces:
@@ -274,11 +270,10 @@
         else:
             pl.loop(first, last)(body)
 
-    repeat(1, groups // 2, collect)
     repeat(0, groups, drain)
     repeat(1, groups, drain_z)
-    repeat(0, groups // 2, lambda j: near_copy(j).wait_send())
-    repeat(1, groups // 2, lambda j: far_copy(j).wait_send())
+    repeat(1, groups, lambda k: share_copy(k).wait())
+    load(own_share, own_hbm, 6).wait()
 
 
 def local(spectra, block_site, live_traces, taper_class, taper_table, operator):
@@ -288,13 +283,15 @@
     depth = operator.shape[1] // PIECES
     receivers = operator.shape[2]
     rows = columns * 2 * shots
-    halves = groups // 2
     dma = pltpu.SemaphoreType.DMA
-    result = pl.pallas_call(
+    own, incoming = pl.pallas_call(
         functools.partial(kernel, groups, columns),
-        out_shape=jax.ShapeDtypeStruct((rows, receivers), jnp.float32),
+        out_shape=(
+            jax.ShapeDtypeStruct((rows, receivers), jnp.float32),
+            jax.ShapeDtypeStruct((groups - 1, rows, receivers), jnp.bfloat16),
+        ),
         in_specs=[pl.BlockSpec(memory_space=pl.ANY)] * 6,
-        out_specs=pl.BlockSpec(memory_space=pltpu.VMEM),
+        out_specs=[pl.BlockSpec(memory_space=pl.ANY)] * 2,
         scratch_shapes=[
             pltpu.VMEM(spectra.shape, spectra.dtype),
             pltpu.VMEM(block_site.shape, jnp.int32),
@@ -304,28 +301,25 @@
             pltpu.VMEM(operator.shape, operator.dtype),
             pltpu.VMEM((groups, PIECES, 2 * shots, depth), jnp.bfloat16),
             pltpu.VMEM((groups, PIECES, columns, 2 * shots, depth), jnp.bfloat16),
-            pltpu.VMEM((halves, rows, receivers), jnp.bfloat16),
-            pltpu.VMEM((halves, rows, receivers), jnp.bfloat16),
-            pltpu.VMEM((halves, rows, receivers), jnp.bfloat16),
-            pltpu.VMEM((halves, rows, receivers), jnp.bfloat16),
-            dma((6,)),
+            pltpu.VMEM((groups - 1, rows, receivers), jnp.bfloat16),
+            pltpu.VMEM((rows, receivers), jnp.float32),
+            dma((7,)),
             dma((groups, PIECES)),
             dma((groups, PIECES)),
             dma((groups, PIECES)),
             dma((groups, PIECES)),
             dma((groups, PIECES, 2)),
             dma((groups, PIECES, 2)),
-            dma((halves,)),
-            dma((halves,)),
-            dma((halves,)),
-            dma((halves,)),
+            dma((groups,)),
+            dma((groups,)),
         ],
         compiler_params=pltpu.CompilerParams(
-            collective_id=0, has_side_effects=True, vmem_limit_bytes=48 * 2**20
+            collective_id=0, has_side_effects=True, vmem_limit_bytes=56 * 2**20
         ),
     )(spectra, block_site, live_traces, taper_class, taper_table, operator)
-    result = result.reshape(columns, 2, shots, receivers)
-    return result.transpose(0, 2, 1, 3).reshape(columns * shots, 2, receivers)
+    total = sum((incoming[k].astype(jnp.float32) for k in range(groups - 1)), own)
+    total = total.reshape(columns, 2, shots, receivers)
+    return total.transpose(0, 2, 1, 3).reshape(columns * shots, 2, receivers)
 
 
 def solution(mesh):

time: 33.9 us -> 25.8 us (0.76)
  local copies, waits for them, and re-layouts: 6.64 us -> 0.76 us
  Pallas kernels: 26.9 us -> 23.9 us
  other arithmetic: 0 us -> 1 us
    unnamed x12 -> x0, local copies, waits for them, and re-layouts: 5.88 us -> none
    pallas_call x1, Pallas kernels: 26.9 us -> 23.9 us  [local(): pl.pallas_call(functools.partial(kernel, groups, columns), out_shape=(jax...]
    add x0 -> x1, other arithmetic: none -> 1 us  [local(): sum((incoming[k].astype(jnp.float32) for k in range(groups - 1)), own)]
where the time goes in v2:
time: 25.8 us; the launch traced here: 25.6 us
  Pallas kernels  23.9 us (93%)
  other arithmetic  1 us (4%)
  local copies, waits for them, and re-layouts  0.76 us (3%)
    pallas_call x1, Pallas kernels, local(): pl.pallas_call(functools.partial(kernel, groups, columns), out_shape=(jax...  23.9 us
    add x1, other arithmetic, local(): sum((incoming[k].astype(jnp.float32) for k in range(groups - 1)), own)  1 us
    transpose x1, local copies, waits for them, and re-layouts, local(): return total.transpose(0, 2, 1, 3).reshape(columns * shots, 2, receivers)  0.76 us

profile of v2, /device:TPU:0, one launch (start us, length us, event | category | flops | bytes accessed | tf_op | source)
XLA Modules:
  0.0 25.6 jit_solution(15396722430524957566)
XLA Ops:
  0.0 23.9 %shard_map.64 = (f32[64,512]{1,0:T(8,128)}, bf16[3,64,512]{2,1,0:T(8,128)(2,1)}) custom-call(bf16[8,2,64,128]{3,2,1,0:T(8,128)(2,1)} %spectra_hbm.1, s32[8,64]{1,0:T(8,128)} %site_hbm.1, s32[8,64]{1,0:T(8,128)} %live_hbm.1, s32[8,64]{1,0:T(8,128)} %class_hbm.1, f32[8,128]{1,0:T(8,128)} %table_hbm.1, bf16[2,2048,512]{2,1,0:T(8,128)(2,1)} %operator_hbm.1), custom_call_target="tpu_custom_call" | custom-call | tf_op jit(solution)/shard_map/pallas_call | solution.py:287
  23.9 1.0 %convert_add_fusion = f32[64,512]{1,0:T(8,128)S(1)} fusion(f32[64,512]{1,0:T(8,128)} %get-tuple-element.7, bf16[3,64,512]{2,1,0:T(8,128)(2,1)} %get-tuple-element.8), kind=kLoop, calls=%fused_computation | loop fusion | flops 196608 | bytes 458752 | tf_op jit(solution)/shard_map/add | solution.py:320
  24.9 0.8 %copy.7 = f32[4,8,2,512]{3,2,1,0:T(2,128)} copy(f32[4,8,2,512]{3,1,2,0:T(8,128)S(1)} %bitcast.13) | data formatting | bytes 262144 | tf_op jit(solution)/shard_map/transpose | solution.py:322

commit v3 on v2

--- a/solution.py
+++ b/solution.py
@@ -9,23 +9,20 @@
 
 MESH = pl.DeviceIdType.MESH
 PIECES = 1
-SENDS = (1, 0, 2, 3)
+SPANS = 1
+SENDS = (2, 0, 1, 3)
 STEPS = (
     ("relay", 0, 0),
+    ("arrive", 2, 0),
     ("arrive", 1, 0),
-    ("arrive", 2, 0),
-    ("multiply", 0, 0),
     ("keep", 0, 0),
+    ("relay", 2, 0),
+    ("arrive", 3, 0),
     ("relay", 1, 0),
-    ("arrive", 3, 0),
-    ("relay", 2, 0),
-    ("multiply", 1, 0),
+    ("send", 2, 0),
+    ("relay", 3, 0),
+    ("send", 3, 0),
     ("send", 1, 0),
-    ("relay", 3, 0),
-    ("multiply", 2, 0),
-    ("send", 2, 0),
-    ("multiply", 3, 0),
-    ("send", 3, 0),
 )
 
 
@@ -155,37 +152,42 @@
         x_copy(k, h, across).wait_recv()
         c_copy(k, h, 1, across).start()
 
-    def products(k, h):
-        c_copy(k, h, 0, beside).wait_recv()
-        c_copy(k, h, 1, flip(across, 1, columns)).wait_recv()
-        rows = data[flip(me, k, groups), h].reshape(columns * 2 * shots, depth)
-        at = h * depth
-        return [
-            jnp.dot(rows, operator[d, at : at + depth, :], preferred_element_type=jnp.float32)
-            for d in range(2)
-        ]
-
-    def combine(parts):
-        first, second = [
-            sum(part[d] for part in parts).reshape(columns, 2, shots, receivers) for d in range(2)
-        ]
+    def gathered(k):
+        for h in range(PIECES):
+            c_copy(k, h, 0, beside).wait_recv()
+            c_copy(k, h, 1, flip(across, 1, columns)).wait_recv()
+
+    def share(k, start, width):
+        first = second = 0.0
+        for h in range(PIECES):
+            rows = data[flip(me, k, groups), h].reshape(columns * 2 * shots, depth)
+            steps, some = slice(h * depth, (h + 1) * depth), slice(start, start + width)
+            first += jnp.dot(rows, operator[0, steps, some], preferred_element_type=jnp.float32)
+            second += jnp.dot(rows, operator[1, steps, some], preferred_element_type=jnp.float32)
+        first = first.reshape(columns, 2, shots, width)
+        second = second.reshape(columns, 2, shots, width)
         return jnp.concatenate(
             [(first[:, 0] - second[:, 1])[:, None], (second[:, 0] + first[:, 1])[:, None]], axis=1
-        ).reshape(columns * 2 * shots, receivers)
-
-    def share(k):
-        return combine([products(k, h) for h in range(PIECES)])
-
-    def share_copy(k):
-        return pltpu.make_async_remote_copy(
-            src_ref=share_out.at[k - 1], dst_ref=incoming_hbm.at[k - 1],
-            send_sem=share_send.at[k], recv_sem=share_recv.at[k],
+        ).reshape(columns * 2 * shots, width)
+
+    def finish(k):
+        gathered(k)
+        for part in range(SPANS):
+            send_share(k, part, share(k, part * span, span))
+
+    span = receivers // SPANS
+
+    def share_copy(k, part):
+        window = (k - 1, slice(None), pl.ds(part * span, span))
+        return pltpu.make_async_remote_copy(
+            src_ref=share_out.at[window], dst_ref=incoming_hbm.at[window],
+            send_sem=share_send.at[k, part], recv_sem=share_recv.at[k, part],
             device_id={"shot": flip(me, k, groups)}, device_id_type=MESH,
         )
 
-    def send_share(k, mine):
-        share_out[k - 1] = mine.astype(jnp.bfloat16)
-        share_copy(k).start()
+    def send_share(k, part, mine):
+        share_out[k - 1, :, part * span : (part + 1) * span] = mine.astype(jnp.bfloat16)
+        share_copy(k, part).start()
 
     def keep_share(mine):
         own_share[...] = mine
@@ -198,11 +200,6 @@
 
     pieces = range(PIECES)
     if groups == 4:
-        done = {k: [] for k in range(groups)}
-
-        def multiply(k, h):
-            done[k].append(products(k, h))
-
         for position, k in enumerate(SENDS):
             if k == 0:
                 write(place(me), lambda h: data.at[me, h, column])
@@ -220,14 +217,12 @@
                 arrive(k, h)
             elif step == "relay":
                 relay(k, h)
-            elif step == "multiply":
-                if k == 0 and h == 0:
-                    large.wait()
-                multiply(k, h)
+            elif step == "keep":
+                large.wait()
+                gathered(0)
+                keep_share(share(0, 0, receivers))
             elif step == "send":
-                send_share(k, combine(done[k]))
-            elif step == "keep":
-                keep_share(combine(done[k]))
+                finish(k)
     else:
         pl.semaphore_wait(barrier, groups + 1)
         pl.loop(1, groups)(send_group)
@@ -247,11 +242,9 @@
                 relay(k, h)
 
         large.wait()
-        keep_share(share(0))
-
-        @pl.loop(1, groups)
-        def _(k):
-            send_share(k, share(k))
+        gathered(0)
+        keep_share(share(0, 0, receivers))
+        pl.loop(1, groups)(finish)
 
     def drain(k):
         for h in pieces:
@@ -272,7 +265,8 @@
 
     repeat(0, groups, drain)
     repeat(1, groups, drain_z)
-    repeat(1, groups, lambda k: share_copy(k).wait())
+    for part in range(SPANS):
+        repeat(1, groups, lambda k: share_copy(k, part).wait())
     load(own_share, own_hbm, 6).wait()
 
 
@@ -310,8 +304,8 @@
             dma((groups, PIECES)),
             dma((groups, PIECES, 2)),
             dma((groups, PIECES, 2)),
-            dma((groups,)),
-            dma((groups,)),
+            dma((groups, SPANS)),
+            dma((groups, SPANS)),
         ],
         compiler_params=pltpu.CompilerParams(
             collective_id=0, has_side_effects=True, vmem_limit_bytes=56 * 2**20

time: 25.8 us -> 25.4 us (0.984)
  Pallas kernels: 23.9 us -> 23.3 us
    pallas_call x1, Pallas kernels: 23.9 us -> 23.3 us  [local(): pl.pallas_call(functools.partial(kernel, groups, columns), out_shape=(jax...]
where the time goes in v3:
time: 25.4 us; the launch traced here: 25.1 us
  Pallas kernels  23.3 us (92%)
  other arithmetic  1 us (4%)
  local copies, waits for them, and re-layouts  0.76 us (3%)
    pallas_call x1, Pallas kernels, local(): pl.pallas_call(functools.partial(kernel, groups, columns), out_shape=(jax...  23.3 us
    add x1, other arithmetic, local(): sum((incoming[k].astype(jnp.float32) for k in range(groups - 1)), own)  1 us
    transpose x1, local copies, waits for them, and re-layouts, local(): return total.transpose(0, 2, 1, 3).reshape(columns * shots, 2, receivers)  0.76 us

profile of v3, /device:TPU:0, one launch (start us, length us, event | category | flops | bytes accessed | tf_op | source)
XLA Modules:
  0.0 25.1 jit_solution(13836922070936148472)
XLA Ops:
  0.0 23.3 %shard_map.64 = (f32[64,512]{1,0:T(8,128)}, bf16[3,64,512]{2,1,0:T(8,128)(2,1)}) custom-call(bf16[8,2,64,128]{3,2,1,0:T(8,128)(2,1)} %spectra_hbm.1, s32[8,64]{1,0:T(8,128)} %site_hbm.1, s32[8,64]{1,0:T(8,128)} %live_hbm.1, s32[8,64]{1,0:T(8,128)} %class_hbm.1, f32[8,128]{1,0:T(8,128)} %table_hbm.1, bf16[2,2048,512]{2,1,0:T(8,128)(2,1)} %operator_hbm.1), custom_call_target="tpu_custom_call" | custom-call | tf_op jit(solution)/shard_map/pallas_call | solution.py:281
  23.3 1.0 %convert_add_fusion = f32[64,512]{1,0:T(8,128)S(1)} fusion(f32[64,512]{1,0:T(8,128)} %get-tuple-element.7, bf16[3,64,512]{2,1,0:T(8,128)(2,1)} %get-tuple-element.8), kind=kLoop, calls=%fused_computation | loop fusion | flops 196608 | bytes 458752 | tf_op jit(solution)/shard_map/add | solution.py:314
  24.3 0.8 %copy.7 = f32[4,8,2,512]{3,2,1,0:T(2,128)} copy(f32[4,8,2,512]{3,1,2,0:T(8,128)S(1)} %bitcast.13) | data formatting | bytes 262144 | tf_op jit(solution)/shard_map/transpose | solution.py:316
